TPU v7x, 256 devices: a whole 4x4x8 slice. The times are simulated.
256 devices in a mesh: row: 16 (over y, x), col: 16 (over z, core).
Axes of the slice: x: 4, y: 4, z: 8, core: 2. Of those that a mesh axis runs over, the one named last changes fastest.
Arguments:
- matrix: float32 [24576, 16384], P('row', 'col'), may hold values from -6 to 6
- lower_panel: float32 [256, 24576], P('col', 'row'), may hold values from -0.375 to 0.375
- pivots: int32 [256], replicated, may hold values from 256 to 24575, as said below
Outputs:
- updated: float32 [24576, 16384], P('row', 'col')
Inputs may be any that keep to these rules, and one draw needn't show every extreme that they name: `pivots`: distinct row ids, each at least 256; the largest and smallest allowed values occur in every draw.
All inputs are finite; a program needn't handle non-finite values.
Results may differ from a plain program's by a relative error of at most 0.0001.
Values sent between devices are 32-bit elements; how exact they have to be, the bound alone decides.
A program may use at most 64 MiB of HBM per device.

v0:
```python
import jax
import jax.numpy as jnp
from jax import lax
from jax.sharding import PartitionSpec as P

NB = 256


def from_root(block, axis, source):
    block = jnp.where(lax.axis_index(axis) == source, block, jnp.zeros_like(block))
    return lax.psum(block, axis)


def multiply(left_side, right_side):
    return jnp.dot(
        left_side, right_side, preferred_element_type=jnp.float32, precision=lax.Precision.HIGHEST
    )


def contract(columns, u_piece):
    return lax.dot_general(
        columns,
        u_piece,
        (((0,), (0,)), ((), ())),
        precision=lax.Precision.HIGHEST,
        preferred_element_type=jnp.float32,
    )


def block_inverse(diag_block):
    strict = jnp.tril(diag_block, -1)
    identity = jnp.eye(diag_block.shape[0], dtype=jnp.float32)
    result = identity - strict
    powered = strict
    for repeat in range(4):
        powered = multiply(powered, powered)
        result = multiply(result, identity + powered)
    return result


def unit_lower_solve(triangle, right_side):
    block_rows = 32
    solved = []
    for offset in range(0, triangle.shape[0], block_rows):
        target = right_side[offset : offset + block_rows]
        if offset > 0:
            target = target - multiply(
                triangle[offset : offset + block_rows, :offset], jnp.concatenate(solved, axis=0)
            )
        solved.append(
            multiply(
                block_inverse(triangle[offset : offset + block_rows, offset : offset + block_rows]),
                target,
            )
        )
    return jnp.concatenate(solved, axis=0)


def body(matrix, lower_panel, pivots):
    rows_dev = matrix.shape[0]
    row_index = lax.axis_index("row")
    first_row = row_index * rows_dev
    top_index = jnp.arange(NB, dtype=jnp.int32)
    offsets = jnp.concatenate([pivots, top_index]) - first_row
    owned_mask = (offsets >= 0) & (offsets < rows_dev)
    fetched = matrix[jnp.clip(offsets, 0, rows_dev - 1)]
    moved_rows = lax.psum(jnp.where(owned_mask[:, None], fetched, 0.0), "row")
    top_rows = moved_rows[:NB]
    old_top = moved_rows[NB:]
    dest_rows = jnp.concatenate([top_index, pivots]) - first_row
    mine_mask = (dest_rows >= 0) & (dest_rows < rows_dev)
    slot_rows = jnp.where(mine_mask, dest_rows, rows_dev)
    swapped = matrix.at[slot_rows].set(jnp.concatenate([top_rows, old_top], axis=0), mode="drop")
    triangle = lax.all_gather(lower_panel[:, :NB], "col", axis=0, tiled=True)
    u_rows = unit_lower_solve(jnp.transpose(triangle), top_rows)
    u_rows = from_root(u_rows, "row", 0)
    whole_panel = lax.all_gather(lower_panel, "col", axis=0, tiled=True)
    updated = swapped - contract(whole_panel, u_rows)
    head_rows = jnp.where(row_index == 0, u_rows, updated[:NB])
    return lax.dynamic_update_slice_in_dim(updated, head_rows, 0, 0)


def solution(mesh):
    placed = (P("row", "col"), P("col", "row"), P())
    return jax.shard_map(
        body, mesh=mesh, in_specs=placed, out_specs=P("row", "col"), check_vma=False
    )
```

profile of v0, /device:TPU:1, one launch (start us, length us, event | category | flops | bytes accessed | tf_op | source)
XLA Modules:
  0.0 250.5 jit_solution(8561862720757232630)
XLA Ops:
  7.4 6.6 %copy.38 = f32[1536,1024]{1,0:T(8,128)} copy(f32[1536,1024]{1,0:T(8,128)} %param.3) | data formatting | bytes 12582912
  14.1 5.6 %gather_fusion = f32[512,1024]{1,0:T(8,128)S(1)} fusion(f32[1536,1024]{1,0:T(8,128)} %copy.38, s32[1024]{0:T(1024)S(1)} %pad_clamp_fusion), kind=kCustom, calls=%fused_computation | custom fusion | bytes 4196352 | tf_op jit(solution)/shard_map/gather | solution.py:66
  19.7 1.5 broadcast_select_fusion
  21.3 0.5 all-gather.2.cloned.1.call-update
  21.9 0.7 slice.86
  22.6 22.0 %all_gather.6 = f32[256,256]{1,0:T(8,128)S(1)} all-gather(f32[16,256]{1,0:T(8,128)S(1)} %slice.86), channel_id=1, replica_groups=mesh['row'=16,'col'=16] {'col'}, dimensions={0}, use_global_device_ids=true | all-gather | bytes 278528 | tf_op jit(solution)/shard_map/all_gather | solution.py:74
  55.4 69.3 %all-reduce.3.cloned.1.call-done = f32[512,1024]{1,0:T(8,128)} async-done(((f32[512,1024]{1,0:T(8,128)}), f32[512,1024]{1,0:T(8,128)}) %all-reduce.3.cloned.1.call-update) | async-done | bytes 2097168 | tf_op jit(solution)/shard_map/psum | solution.py:67
  124.7 1.3 constant_dynamic-update-slice_fusion.17
  126.0 1.2 fusion.5
  127.2 0.3 constant_dynamic-update-slice_fusion.16
  127.4 1.2 fusion.6
  128.6 0.3 constant_dynamic-update-slice_fusion.15
  128.9 0.3 fusion.4
  129.3 0.3 constant_dynamic-update-slice_fusion.14
  129.6 0.4 fusion.3
  130.0 0.3 constant_dynamic-update-slice_fusion.13
  130.3 0.5 fusion.2
  131.0 0.6 fusion.1
  131.8 0.7 fusion
  132.8 1.1 broadcast_select_fusion.1
  133.9 7.7 %scatter_fusion = f32[1536,1024]{1,0:T(8,128)} fusion(f32[1536,1024]{1,0:T(8,128)} %copy.38, s32[512]{0:T(512)S(1)} %bitcast.158, f32[512,1024]{1,0:T(8,128)S(1)} %copy-done.1), kind=kCustom, calls=%fused_computation.1 | custom fusion | bytes 6293504 | tf_op jit(solution)/shard_map/scatter | solution.py:73
  141.6 88.6 %all-reduce.5.cloned.1.call-done = f32[256,1024]{1,0:T(8,128)} async-done(((f32[256,1024]{1,0:T(8,128)}), f32[256,1024]{1,0:T(8,128)}) %all-reduce.5.cloned.1.call-update) | async-done | bytes 1048592 | tf_op jit(solution)/shard_map/psum | solution.py:11
  230.2 10.4 %bitcast_subtract_fusion = f32[1536,1024]{1,0:T(8,128)} fusion(f32[1536,1024]{1,0:T(8,128)} %scatter_fusion, f32[256,1024]{1,0:T(8,128)} %all-reduce.5.cloned.1.call-done, f32[256,1536]{1,0:T(8,128)} %all-gather.2.cloned.1.call-done), kind=kOutput, calls=%fused_computation.2 | convolution fusion | flops 4833411072 | bytes 15204352 | tf_op jit(solution)/shard_map/dot_general | solution.py:21
  240.7 2.3 fusion.7
  (87 shorter events, 11.5 us)
Async XLA Ops:
  7.4 6.6 %copy-start.2 = (s32[256]{0:T(256)S(1)}, s32[256]{0:T(256)}, u32[]{:S(2)}) copy-start(s32[256]{0:T(256)} %param.5) | copy-start | bytes 3076
  7.4 117.3 %all-reduce.3.cloned.1.call-start = ((), (), s32[]{:S(2)}) async-start(), calls=%async_computation | async-start | bytes 4194304 | tf_op jit(solution)/shard_map/psum | solution.py:67
  21.2 120.4 %all-gather.2.cloned.1.call-start = ((), (), s32[]{:S(2)}) async-start(), calls=%async_computation.2 | async-start | bytes 1671168 | tf_op jit(solution)/shard_map/all_gather | solution.py:77
  21.8 208.4 %all-reduce.5.cloned.1.call-start = ((), (), s32[]{:S(2)}) async-start(), calls=%async_computation.1 | async-start | bytes 2097152 | tf_op jit(solution)/shard_map/psum | solution.py:11
  124.7 4.3 %copy-start.1 = (f32[512,1024]{1,0:T(8,128)S(1)}, f32[512,1024]{1,0:T(8,128)}, u32[]{:S(2)}) copy-start(f32[512,1024]{1,0:T(8,128)} %all-reduce.3.cloned.1.call-done) | copy-start | bytes 6291460
  230.2 10.4 %copy-start = (f32[256,1024]{1,0:T(8,128)S(1)}, f32[256,1024]{1,0:T(8,128)}, u32[]{:S(2)}) copy-start(f32[256,1024]{1,0:T(8,128)} %all-reduce.5.cloned.1.call-done) | copy-start | bytes 3145732
Sparse Core Ops, SparseCore 0:
  21.4 103.2 all-reduce.2
  134.0 96.1 all-reduce.4
Sparse Core Ops, SparseCore 1:
  23.7 43.4 all-gather.1
where the time goes:
time: 251 us; the launch traced here: 250 us
  waiting for transfers between devices  158 us (63%)
  matrix products  28.9 us (12%)
  blocking collectives  22 us (9%)
  local copies, waits for them, and re-layouts  20.8 us (8%)
  between operations  15.2 us (6%)
  other arithmetic  5.01 us (2%)
    psum x1, waiting for transfers between devices, from_root(): return lax.psum(block, axis)  88.6 us
    psum x1, waiting for transfers between devices, body(): moved_rows = lax.psum(jnp.where(owned_mask[:, None], fetched, 0.0), 'row')  69.3 us
    all_gather x1, blocking collectives, body(): triangle = lax.all_gather(lower_panel[:, :NB], 'col', axis=0, tiled=True)  22 us
    dot_general x79, matrix products, multiply(): jnp.dot(left_side, right_side, preferred_element_type=jnp.float32, precis...  18.4 us
    dot_general x1, matrix products, contract(): lax.dot_general(columns, u_piece, (((0,), (0,)), ((), ())), precision=lax...  10.4 us
    scatter x1, local copies, waits for them, and re-layouts, body(): matrix.at[slot_rows]  7.69 us
    unnamed x7, local copies, waits for them, and re-layouts  6.63 us
    gather x1, local copies, waits for them, and re-layouts, body(): fetched = matrix[jnp.clip(offsets, 0, rows_dev - 1)]  5.61 us
  transfers between devices with their start and end apart: 3, of which 2 were waited for; matrix products, arithmetic and copies ran while one was open for 11% of the time, Pallas kernels for 0%

commit v1 on v0

v1 whole, which is shorter than its diff:
```python
import jax
import jax.numpy as jnp
from jax import lax
from jax.experimental import pallas as pl
from jax.experimental.pallas import tpu as pltpu
from jax.sharding import PartitionSpec as P

NB = 256
ROWS = 1536
COLS = 1024
HALF = 512
MESH = pl.DeviceIdType.MESH
F32 = jnp.float32
BF16 = jnp.bfloat16


def exact(a, b):
    return jnp.dot(a, b, preferred_element_type=F32, precision=lax.Precision.HIGHEST)


def upper_inverse(tri):
    i = lax.broadcasted_iota(jnp.int32, (NB, NB), 0)
    j = lax.broadcasted_iota(jnp.int32, (NB, NB), 1)
    eye = jnp.where(i == j, 1.0, 0.0).astype(F32)
    power = jnp.where((j > i) & (i // 32 == j // 32), tri, 0.0)
    inv = eye - power
    for _ in range(4):
        power = exact(power, power)
        inv = exact(inv, eye + power)
    for size in (32, 64, 128):
        block = (i // (2 * size) == j // (2 * size)) & (i // size < j // size)
        inv = inv - exact(exact(inv, jnp.where(block, tri, 0.0)), inv)
    return inv


def exchange_kernel(
    piv, mat_hbm, panel, top, old, w_hi, w_lo,
    mat, sel, r1a, r1b, r2a, r2b, pa, pb, pan, tri, inv,
    mat_sem, p1s, p1r, p2s, p2r, p3s, p3r, p4s, p4r, scs, scr, tbs, tbr,
    tzs, tzr, tcs, tcr, pzs, pzr, pcs, pcr,
):
    r = lax.axis_index("row")
    c = lax.axis_index("col")
    y, x = r // 4, r % 4
    z, k = c // 2, c % 2
    is_root = r == 0

    head = pltpu.make_async_copy(mat_hbm.at[pl.ds(0, NB)], mat.at[pl.ds(0, NB)], mat_sem.at[0])
    rest = pltpu.make_async_copy(mat_hbm.at[pl.ds(NB, ROWS - NB)], mat.at[pl.ds(NB, ROWS - NB)], mat_sem.at[1])
    head.start()
    rest.start()

    def rowdev(yy, xx):
        return (yy * 4 + xx, c)

    def coldev(zz, kk):
        return (r, zz * 2 + kk)

    barrier = pltpu.get_barrier_semaphore()
    for d in range(1, 16):
        pl.semaphore_signal(barrier, inc=1, device_id=((r + d) % 16, c), device_id_type=MESH)
    for d in range(1, 8):
        pl.semaphore_signal(barrier, inc=1, device_id=coldev((z + d) % 8, k), device_id_type=MESH)
    pl.semaphore_signal(barrier, inc=1, device_id=coldev(z, 1 - k), device_id_type=MESH)
    pl.semaphore_wait(barrier, 23)

    def remote(src, dst, ss, rs, dev):
        return pltpu.make_async_remote_copy(
            src_ref=src, dst_ref=dst, send_sem=ss, recv_sem=rs, device_id=dev, device_id_type=MESH
        )

    def piece(ref, zz, kk):
        return ref.at[pl.ds(pl.multiple_of((zz * 2 + kk) * 16, 16), 16)]

    mine = piece(tri, z, k)
    tri_bcast = [
        remote(panel.at[:, pl.ds(0, NB)], mine, tbs.at[d - 1], tbr.at[0], ((r + d) % 16, c)) for d in range(1, 16)
    ]

    @pl.when(is_root)
    def _():
        for cp in tri_bcast:
            cp.start()
        tri[pl.ds(pl.multiple_of(c * 16, 16), 16), :] = panel[:, :NB]

    pan[pl.ds(pl.multiple_of(c * 16, 16), 16), :] = panel[...]
    pan_z = [
        remote(panel, piece(pan, z, k), pzs.at[d - 1], pzr.at[d - 1], coldev((z + d) % 8, k)) for d in range(1, 8)
    ]
    pan_core = [
        remote(
            panel if d == 0 else piece(pan, (z + 8 - d) % 8, k),
            piece(pan, (z + 8 - d) % 8, k),
            pcs.at[d], pcr.at[d], coldev(z, 1 - k),
        )
        for d in range(8)
    ]
    order = (1, 7, 2, 6, 3, 5, 4)
    for d in order:
        pan_z[d - 1].start()
    pan_core[0].start()

    head.wait()
    ca = pl.ds(0, HALF)
    cb = pl.ds(HALF, HALF)

    def rows_a(yy, xx):
        return pl.ds(pl.multiple_of(xx * 64 + yy * 16, 16), 16)

    def rows_b(yy, xx):
        return pl.ds(pl.multiple_of(yy * 64 + xx * 16, 16), 16)

    scatter = []
    for d in range(1, 16):
        rr = (r + d) % 16
        yy, xx = rr // 4, rr % 4
        at = (rows_a(yy, xx), ca)
        bt = (rows_b(yy, xx), cb)
        scatter.append(remote(mat.at[at], old.at[at], scs.at[2 * d - 2], scr.at[0], (rr, c)))
        scatter.append(remote(mat.at[bt], old.at[bt], scs.at[2 * d - 1], scr.at[1], (rr, c)))

    @pl.when(is_root)
    def _():
        for cp in scatter:
            cp.start()
        old[rows_a(y, x), ca] = mat[rows_a(y, x), ca]
        old[rows_b(y, x), cb] = mat[rows_b(y, x), cb]

    rest.wait()
    first = r * ROWS

    def pick(g, carry):
        for i in range(8):
            off = piv[g * 8 + i] - first
            own = (off >= 0) & (off < ROWS)
            row = mat[pl.ds(jnp.clip(off, 0, ROWS - 1), 1), :]
            sel[pl.ds(g * 8 + i, 1), :] = jnp.where(own, row, 0.0)
        return carry

    lax.fori_loop(0, NB // 8, pick, 0)

    def r64(i):
        return pl.ds(pl.multiple_of(i * 64, 64), 64)

    def r16(i):
        return pl.ds(pl.multiple_of(i * 16, 16), 16)

    p1 = []
    for d in (1, 3, 2):
        xx, yy = (x + d) % 4, (y + d) % 4
        p1.append(remote(sel.at[r64(xx), ca], r1a.at[d - 1], p1s.at[d - 1], p1r.at[d - 1], rowdev(y, xx)))
        p1.append(remote(sel.at[r64(yy), cb], r1b.at[d - 1], p1s.at[d + 2], p1r.at[d + 2], rowdev(yy, x)))
    for cp in p1:
        cp.start()

    tri_z = [
        remote(mine, mine, tzs.at[d - 1], tzr.at[d - 1], coldev((z + d) % 8, k)) for d in range(1, 8)
    ]
    tri_core = [
        remote(
            piece(tri, (z + 8 - d) % 8, k), piece(tri, (z + 8 - d) % 8, k),
            tcs.at[d], tcr.at[d], coldev(z, 1 - k),
        )
        for d in range(8)
    ]

    @pl.when(jnp.logical_not(is_root))
    def _():
        tri_bcast[0].wait_recv()

    for d in order:
        tri_z[d - 1].start()
    tri_core[0].start()

    for cp in p1:
        cp.wait_recv()
    pa[...] = sel[r64(x), ca] + r1a[0] + r1a[1] + r1a[2]
    pb[...] = sel[r64(y), cb] + r1b[0] + r1b[1] + r1b[2]
    p2 = []
    for d in (1, 3, 2):
        xx, yy = (x + d) % 4, (y + d) % 4
        p2.append(remote(pa.at[r16(yy)], r2a.at[d - 1], p2s.at[d - 1], p2r.at[d - 1], rowdev(yy, x)))
        p2.append(remote(pb.at[r16(xx)], r2b.at[d - 1], p2s.at[d + 2], p2r.at[d + 2], rowdev(y, xx)))
    for cp in p2:
        cp.start()

    for d in order:
        tri_z[d - 1].wait_recv()
        tri_core[d].start()

    for cp in p2:
        cp.wait_recv()
    top[rows_a(y, x), ca] = pa[r16(y), :] + r2a[0] + r2a[1] + r2a[2]
    top[rows_b(y, x), cb] = pb[r16(x), :] + r2b[0] + r2b[1] + r2b[2]

    @pl.when(jnp.logical_not(is_root))
    def _():
        scatter[0].wait_recv()
        scatter[1].wait_recv()

    p3 = []
    for w, ref in enumerate((top, old)):
        at = ref.at[rows_a(y, x), ca]
        bt = ref.at[rows_b(y, x), cb]
        for d in (1, 3, 2):
            xx, yy = (x + d) % 4, (y + d) % 4
            n = w * 6 + d - 1
            p3.append(remote(at, at, p3s.at[n], p3r.at[n], rowdev(yy, x)))
            p3.append(remote(bt, bt, p3s.at[n + 3], p3r.at[n + 3], rowdev(y, xx)))
    for cp in p3:
        cp.start()
    for cp in p3:
        cp.wait_recv()

    p4 = []
    for w, ref in enumerate((top, old)):
        at = ref.at[r64(x), ca]
        bt = ref.at[r64(y), cb]
        for d in (1, 3, 2):
            xx, yy = (x + d) % 4, (y + d) % 4
            n = w * 6 + d - 1
            p4.append(remote(at, at, p4s.at[n], p4r.at[n], rowdev(y, xx)))
            p4.append(remote(bt, bt, p4s.at[n + 3], p4r.at[n + 3], rowdev(yy, x)))
    for cp in p4:
        cp.start()

    for d in order:
        pan_z[d - 1].wait_recv()
        pan_core[d].start()

    for d in range(8):
        tri_core[d].wait_recv()
    inv[...] = upper_inverse(tri[...])
    for d in range(8):
        pan_core[d].wait_recv()

    for m in range(ROWS // NB):
        w = exact(inv[...], pan[:, m * NB : (m + 1) * NB])
        if m == 0:
            w = jnp.where(is_root, -inv[...], w)
        w = jnp.transpose(w)
        hi = w.astype(BF16)
        w_hi[m * NB : (m + 1) * NB, :] = hi
        w_lo[m * NB : (m + 1) * NB, :] = (w - hi.astype(F32)).astype(BF16)

    for cp in p4:
        cp.wait_recv()
    for cp in p1 + p2 + p3 + p4 + pan_z + pan_core + tri_z + tri_core:
        cp.wait_send()

    @pl.when(is_root)
    def _():
        for cp in tri_bcast + scatter:
            cp.wait_send()


def exchange(pivots, matrix, panel):
    vmem = pl.BlockSpec(memory_space=pltpu.VMEM)
    dma = pltpu.SemaphoreType.DMA
    return pl.pallas_call(
        exchange_kernel,
        out_shape=(
            jax.ShapeDtypeStruct((NB, COLS), F32),
            jax.ShapeDtypeStruct((NB, COLS), F32),
            jax.ShapeDtypeStruct((ROWS, NB), BF16),
            jax.ShapeDtypeStruct((ROWS, NB), BF16),
        ),
        in_specs=[pl.BlockSpec(memory_space=pltpu.SMEM), pl.BlockSpec(memory_space=pl.ANY), vmem],
        out_specs=(vmem,) * 4,
        scratch_shapes=[
            pltpu.VMEM((ROWS, COLS), F32),
            pltpu.VMEM((NB, COLS), F32),
            pltpu.VMEM((3, 64, HALF), F32),
            pltpu.VMEM((3, 64, HALF), F32),
            pltpu.VMEM((3, 16, HALF), F32),
            pltpu.VMEM((3, 16, HALF), F32),
            pltpu.VMEM((64, HALF), F32),
            pltpu.VMEM((64, HALF), F32),
            pltpu.VMEM((NB, ROWS), F32),
            pltpu.VMEM((NB, NB), F32),
            pltpu.VMEM((NB, NB), F32),
            dma((2,)),
            dma((6,)), dma((6,)), dma((6,)), dma((6,)),
            dma((12,)), dma((12,)), dma((12,)), dma((12,)),
            dma((30,)), dma((2,)), dma((15,)), dma((1,)),
            dma((7,)), dma((7,)), dma((8,)), dma((8,)),
            dma((7,)), dma((7,)), dma((8,)), dma((8,)),
        ],
        name="exchange",
        compiler_params=pltpu.CompilerParams(
            collective_id=0, has_side_effects=True, vmem_limit_bytes=40 * 1024 * 1024
        ),
    )(pivots, matrix, panel)


TILE = 256


def update_kernel(piv, mat_hbm, top, old, w_hi, w_lo, out_hbm, mat, th, tl, at_row, at_k, count, in_sem, out_sem):
    r = lax.axis_index("row")
    tiles = ROWS // TILE

    def load(t):
        rows = pl.ds(t * TILE, TILE)
        return pltpu.make_async_copy(mat_hbm.at[rows], mat.at[rows], in_sem.at[t])

    def store(t):
        rows = pl.ds(t * TILE, TILE)
        return pltpu.make_async_copy(mat.at[rows], out_hbm.at[rows], out_sem.at[t])

    for t in range(tiles):
        load(t).start()
    first = r * ROWS
    count[0] = 0

    def collect(i, carry):
        off = piv[i] - first

        @pl.when((off >= 0) & (off < ROWS))
        def _():
            n = count[0]
            at_row[n] = off
            at_k[n] = i
            count[0] = n + 1

        return carry

    lax.fori_loop(0, NB, collect, 0)
    hi = top[...].astype(BF16)
    th[...] = hi
    tl[...] = (top[...] - hi.astype(F32)).astype(BF16)
    for t in range(tiles):
        load(t).wait()

    def place(n, carry):
        mat[pl.ds(at_row[n], 1), :] = old[pl.ds(at_k[n], 1), :]
        return carry

    lax.fori_loop(0, count[0], place, 0)

    @pl.when(r == 0)
    def _():
        mat[:NB, :] = jnp.zeros((NB, COLS), F32)

    def dot(a, b):
        return jnp.dot(a, b, preferred_element_type=F32)

    for t in range(tiles):
        rows = pl.ds(t * TILE, TILE)
        a, b = w_hi[rows, :], w_lo[rows, :]
        mat[rows, :] = mat[rows, :] - (dot(a, th[...]) + (dot(b, th[...]) + dot(a, tl[...])))
        store(t).start()
    for t in range(tiles):
        store(t).wait()


def update(pivots, matrix, top, old, w_hi, w_lo):
    vmem = pl.BlockSpec(memory_space=pltpu.VMEM)
    smem = pl.BlockSpec(memory_space=pltpu.SMEM)
    anyspace = pl.BlockSpec(memory_space=pl.ANY)
    return pl.pallas_call(
        update_kernel,
        out_shape=jax.ShapeDtypeStruct((ROWS, COLS), F32),
        in_specs=[smem, anyspace, vmem, vmem, vmem, vmem],
        out_specs=anyspace,
        scratch_shapes=[
            pltpu.VMEM((ROWS, COLS), F32),
            pltpu.VMEM((NB, COLS), BF16),
            pltpu.VMEM((NB, COLS), BF16),
            pltpu.SMEM((NB,), jnp.int32),
            pltpu.SMEM((NB,), jnp.int32),
            pltpu.SMEM((1,), jnp.int32),
            pltpu.SemaphoreType.DMA((6,)),
            pltpu.SemaphoreType.DMA((6,)),
        ],
        name="update",
        compiler_params=pltpu.CompilerParams(vmem_limit_bytes=32 * 1024 * 1024),
    )(pivots, matrix, top, old, w_hi, w_lo)


def body(matrix, lower_panel, pivots):
    top, old, w_hi, w_lo = exchange(pivots, matrix, lower_panel)
    return update(pivots, matrix, top, old, w_hi, w_lo)


def solution(mesh):
    placed = (P("row", "col"), P("col", "row"), P())
    return jax.shard_map(
        body, mesh=mesh, in_specs=placed, out_specs=P("row", "col"), check_vma=False
    )
```

time: 251 us -> 64.5 us (0.26)
  the two profiles are of different devices: /device:TPU:1 before, /device:TPU:2 now
where the time goes in v1:
time: 64.5 us; the launch traced here: 64.3 us
  Pallas kernels  59.9 us (93%)
  local copies, waits for them, and re-layouts  4.36 us (7%)
    pallas_call x1, Pallas kernels, exchange(): pl.pallas_call(exchange_kernel, out_shape=(jax.ShapeDtypeStruct((NB, COLS...  51.9 us
    pallas_call x1, Pallas kernels, update(): pl.pallas_call(update_kernel, out_shape=jax.ShapeDtypeStruct((ROWS, COLS)...  8 us
    unnamed x8, local copies, waits for them, and re-layouts  4.36 us

profile of v1, /device:TPU:2, one launch (start us, length us, event | category | flops | bytes accessed | tf_op | source)
XLA Modules:
  0.0 64.3 jit_solution(12712134026762527928)
XLA Ops:
  0.0 0.0 copy-start
  0.0 2.8 %copy-done = f32[1536,1024]{1,0:T(8,128)S(1)} copy-done((f32[1536,1024]{1,0:T(8,128)S(1)}, f32[1536,1024]{1,0:T(8,128)}, u32[]{:S(2)}) %copy-start) | copy-done | bytes 6291480
  2.8 0.0 copy-start.2
  2.8 0.9 %copy-done.2 = f32[16,1536]{1,0:T(8,128)S(1)} copy-done((f32[16,1536]{1,0:T(8,128)S(1)}, f32[16,1536]{1,0:T(8,128)}, u32[]{:S(2)}) %copy-start.2) | copy-done | bytes 98328
  3.7 0.0 copy-start.3
  3.7 0.7 %copy-done.3 = s32[256]{0:T(256)S(1)} copy-done((s32[256]{0:T(256)S(1)}, s32[256]{0:T(256)}, u32[]{:S(2)}) %copy-start.3) | copy-done | bytes 1048
  4.4 0.0 copy-start.1
  4.4 51.9 %exchange.1 = (f32[256,1024]{1,0:T(8,128)S(1)}, f32[256,1024]{1,0:T(8,128)S(1)}, bf16[1536,256]{1,0:T(8,128)(2,1)S(1)}, bf16[1536,256]{1,0:T(8,128)(2,1)S(1)}) custom-call(s32[256]{0:T(256)S(1)} %copy-done.3, f32[1536,1024]{1,0:T(8,128)S(1)} %copy-done, f32[16,1536]{1,0:T(8,128)S(1)} %copy-done.2), custom_call_target="tpu_custom_call" | custom-call | tf_op jit(solution)/shard_map/exchange/pallas_call | solution.py:260
  56.3 0.0 copy-done.1
  56.3 8.0 %update.1 = f32[1536,1024]{1,0:T(8,128)} custom-call(s32[256]{0:T(256)S(1)} %copy-done.3, f32[1536,1024]{1,0:T(8,128)S(1)} %copy-done.1, f32[256,1024]{1,0:T(8,128)S(1)} %get-tuple-element.9.top, f32[256,1024]{1,0:T(8,128)S(1)} %get-tuple-element.10.old, bf16[1536,256]{1,0:T(8,128)(2,1)S(1)} %get-tuple-element.11.w_hi, ...), custom_call_target="tpu_custom_call" | custom-call | tf_op jit(solution)/shard_map/update/pallas_call | solution.py:361
Async XLA Ops:
  0.0 2.8 %copy-start = (f32[1536,1024]{1,0:T(8,128)S(1)}, f32[1536,1024]{1,0:T(8,128)}, u32[]{:S(2)}) copy-start(f32[1536,1024]{1,0:T(8,128)} %mat_hbm.3) | copy-start | bytes 18874372
  2.8 0.9 %copy-start.2 = (f32[16,1536]{1,0:T(8,128)S(1)}, f32[16,1536]{1,0:T(8,128)}, u32[]{:S(2)}) copy-start(f32[16,1536]{1,0:T(8,128)} %panel.1) | copy-start | bytes 294916
  3.7 0.7 %copy-start.3 = (s32[256]{0:T(256)S(1)}, s32[256]{0:T(256)}, u32[]{:S(2)}) copy-start(s32[256]{0:T(256)} %piv.3) | copy-start | bytes 3076
  4.4 52.0 %copy-start.1 = (f32[1536,1024]{1,0:T(8,128)S(1)}, f32[1536,1024]{1,0:T(8,128)}, u32[]{:S(2)}) copy-start(f32[1536,1024]{1,0:T(8,128)} %mat_hbm.3) | copy-start | bytes 18874372

commit v2 on v0

v2 whole, which is shorter than its diff:
```python
import functools

import jax
import jax.numpy as jnp
from jax import lax
from jax.experimental import pallas as pl
from jax.experimental.pallas import tpu as pltpu
from jax.sharding import PartitionSpec as P

NB = 256
ROWS = 1536
COLS = 1024
HALF = 512
MESH = pl.DeviceIdType.MESH
F32 = jnp.float32
BF16 = jnp.bfloat16


def exact(a, b):
    return jnp.dot(a, b, preferred_element_type=F32, precision=lax.Precision.HIGHEST)


def inverse_stages(tri, power, inv):
    i = lax.broadcasted_iota(jnp.int32, (NB, NB), 0)
    j = lax.broadcasted_iota(jnp.int32, (NB, NB), 1)
    eye = jnp.where(i == j, 1.0, 0.0).astype(F32)

    def begin():
        power[...] = jnp.where((j > i) & (i // 32 == j // 32), tri[...], 0.0)
        inv[...] = eye - power[...]

    def square():
        squared = exact(power[...], power[...])
        power[...] = squared
        inv[...] = exact(inv[...], eye + squared)

    def double(size):
        block = (i // (2 * size) == j // (2 * size)) & (i // size < j // size)
        inv[...] = inv[...] - exact(exact(inv[...], jnp.where(block, tri[...], 0.0)), inv[...])

    steps = [begin, square, square, square, square]
    return steps + [functools.partial(double, size) for size in (32, 64, 128)]


SUB = 2
WIDE = HALF // SUB


def exchange_kernel(
    piv_hbm, mat_hbm, panel_hbm, mat, mix, top_hi, top_lo, w_hi, w_lo,
    piv, owner, sel, r1a, r1b, r2a, r2b, pa, pb, ga, gb, sa, sb, both_a, both_b, m4a, m4b, pan, tri, power, inv,
    in_sem, p1s, p1r, p2s, p2r, p3s, p3r, p4s, p4r, tbs, tbr,
    tzs, tzr, tcs, tcr, pzs, pzr, pcs, pcr,
):
    r = lax.axis_index("row")
    c = lax.axis_index("col")
    y, x = r // 4, r % 4
    z, k = c // 2, c % 2
    is_root = r == 0

    def piece(ref, zz, kk):
        return ref.at[pl.ds(pl.multiple_of((zz * 2 + kk) * 16, 16), 16)]

    my_pan = piece(pan, z, k)
    my_tri = piece(tri, z, k)
    load_pan = pltpu.make_async_copy(panel_hbm, my_pan, in_sem.at[0])
    load_piv = pltpu.make_async_copy(piv_hbm, piv, in_sem.at[1])
    load_mat = pltpu.make_async_copy(mat_hbm, mat, in_sem.at[2])
    load_pan.start()
    load_piv.start()
    load_mat.start()

    def rowdev(yy, xx):
        return (yy * 4 + xx, c)

    def coldev(zz, kk):
        return (r, zz * 2 + kk)

    barrier = pltpu.get_barrier_semaphore()
    for d in range(1, 4):
        pl.semaphore_signal(barrier, inc=1, device_id=rowdev(y, (x + d) % 4), device_id_type=MESH)
        pl.semaphore_signal(barrier, inc=1, device_id=rowdev((y + d) % 4, x), device_id_type=MESH)
    for d in range(1, 8):
        pl.semaphore_signal(barrier, inc=1, device_id=coldev((z + d) % 8, k), device_id_type=MESH)
    pl.semaphore_signal(barrier, inc=1, device_id=coldev(z, 1 - k), device_id_type=MESH)
    pl.semaphore_wait(barrier, 14)

    def remote(src, dst, ss, rs, dev):
        return pltpu.make_async_remote_copy(
            src_ref=src, dst_ref=dst, send_sem=ss, recv_sem=rs, device_id=dev, device_id_type=MESH
        )

    def r64(i):
        return pl.ds(pl.multiple_of(i * 64, 64), 64)

    def r16(i):
        return pl.ds(pl.multiple_of(i * 16, 16), 16)

    def group(outer, inner):
        return pl.ds(pl.multiple_of(outer * 64 + inner * 16, 16), 16)

    near = (1, 3, 2)

    load_pan.wait()
    tri_x = [
        remote(my_pan.at[:, pl.ds(0, NB)], my_tri, tbs.at[d - 1], tbr.at[0], rowdev(y, (x + d) % 4)) for d in range(1, 4)
    ]
    tri_y = [remote(my_tri, my_tri, tbs.at[d + 2], tbr.at[1], rowdev((y + d) % 4, x)) for d in range(1, 4)]

    @pl.when(is_root)
    def _():
        for cp in tri_x:
            cp.start()
        mine = pl.ds(pl.multiple_of(c * 16, 16), 16)
        tri[mine, :] = pan[mine, :NB]

    def column(ref, zs, zr, cs, cr):
        mine = piece(ref, z, k)
        along = {d: remote(mine, mine, zs.at[d - 1], zr.at[d - 1], coldev((z + d) % 8, k)) for d in range(1, 8)}
        across = []
        for d in range(8):
            got = piece(ref, (z + 8 - d) % 8, k)
            across.append(remote(got, got, cs.at[d], cr.at[d], coldev(z, 1 - k)))
        return along, across

    tri_z, tri_core = column(tri, tzs, tzr, tcs, tcr)
    pan_z, pan_core = column(pan, pzs, pzr, pcs, pcr)
    early, late = (1, 7, 2, 6), (3, 5, 4)
    order = early + late
    for d in early:
        pan_z[d].start()
    pan_core[0].start()

    load_piv.wait()
    load_mat.wait()
    first = r * ROWS

    def pick(g, carry):
        for i in range(8):
            at = pl.ds(g * 8 + i, 1)
            pivot = piv[g * 8 + i]
            off = pivot - first
            own = (off >= 0) & (off < ROWS)
            row = mat[pl.ds(jnp.clip(off, 0, ROWS - 1), 1), :]
            sel[at, :] = jnp.where(own, row, jnp.where(is_root, mat[at, :], 0.0))
            owner[at, :] = jnp.full((1, WIDE), ((pivot >> 9) * 43691) >> 17, jnp.int32)
        return carry

    lax.fori_loop(0, NB // 8, pick, 0)

    def ca(s):
        return pl.ds(s * WIDE, WIDE)

    def cb(s):
        return pl.ds(HALF + s * WIDE, WIDE)

    def around(s, ss, rs, part_a, part_b, a_along_x):
        copies = []
        for d in near:
            xx, yy = (x + d) % 4, (y + d) % 4
            at, bt = s * 6 + d - 1, s * 6 + d + 2
            to_x, to_y = rowdev(y, xx), rowdev(yy, x)
            src, dst = part_a(xx if a_along_x else yy, d - 1)
            copies.append(remote(src, dst, ss.at[at], rs.at[at], to_x if a_along_x else to_y))
            src, dst = part_b(yy if a_along_x else xx, d - 1)
            copies.append(remote(src, dst, ss.at[bt], rs.at[bt], to_y if a_along_x else to_x))
        return copies

    def start(copies):
        for cp in copies:
            cp.start()

    def arrive(copies):
        for cp in copies:
            cp.wait_recv()

    p1, p2, p3, p4 = [], [], [], []
    for s in range(SUB):
        p1.append(around(
            s, p1s, p1r,
            lambda to, d: (sel.at[r64(to), ca(s)], r1a.at[s, d]),
            lambda to, d: (sel.at[r64(to), cb(s)], r1b.at[s, d]), True))
        p2.append(around(
            s, p2s, p2r,
            lambda to, d: (sa.at[s, r16(to)], r2a.at[s, d]),
            lambda to, d: (sb.at[s, r16(to)], r2b.at[s, d]), False))
        p3.append(around(
            s, p3s, p3r,
            lambda to, d: (both_a.at[s, y],) * 2,
            lambda to, d: (both_b.at[s, x],) * 2, False))
        p4.append(around(
            s, p4s, p4r,
            lambda to, d: (m4a.at[s, d], mix.at[r64(x), ca(s)]),
            lambda to, d: (m4b.at[s, d], mix.at[r64(y), cb(s)]), True))
        start(p1[s])

    def total(parts, here, foreign):
        out = None
        for i, part in enumerate(parts):
            part = jnp.where(here == i, jnp.where(foreign, 0.0, part), part)
            out = part if out is None else out + part
        return out

    def one_of(parts, here):
        out = parts[3]
        for i in (2, 1, 0):
            out = jnp.where(here == i, parts[i], out)
        return out

    def add_one(s):
        arrive(p1[s])
        for cols, along, across, got, part, group_old, send, is_line in (
            (ca(s), x, y, r1a, pa, ga, sa, lambda dev: dev >> 2),
            (cb(s), y, x, r1b, pb, gb, sb, lambda dev: dev & 3),
        ):
            dev = owner[r64(along), :]
            parts = [sel[r64(along), cols], got[s, 0], got[s, 1], got[s, 2]]
            summed = total(parts, jnp.where(across == 0, along, -1), dev != 0)
            old = one_of(parts, along)
            part[s] = summed
            group_old[s] = old
            send[s] = jnp.where(is_line(dev) == 0, summed, jnp.where(across == 0, old, summed))
        start(p2[s])

    def add_two(s):
        arrive(p2[s])
        for along, across, got, part, group_old, both, is_line in (
            (x, y, r2a, pa, ga, both_a, lambda dev: dev >> 2),
            (y, x, r2b, pb, gb, both_b, lambda dev: dev & 3),
        ):
            dev = owner[group(along, across), :]
            parts = [part[s, r16(across), :], got[s, 0], got[s, 1], got[s, 2]]
            both[s, across, 0] = total(parts, jnp.where(across == 0, -1, across), is_line(dev) != 0)
            both[s, across, 1] = one_of([group_old[s, r16(across), :], parts[1], parts[2], parts[3]], across)
        start(p3[s])

    def last(s):
        arrive(p3[s])
        for cols, along, across, both, group_old, send, number in (
            (ca(s), x, y, both_a, ga, m4a, lambda to: y * 4 + to),
            (cb(s), y, x, both_b, gb, m4b, lambda to: to * 4 + x),
        ):
            dev = owner[r64(along), :]
            new = both[s, :, 0].reshape(64, WIDE)
            old = jnp.where(across == 0, group_old[s], both[s, :, 1].reshape(64, WIDE))
            for d in near:
                send[s, d - 1] = jnp.where(dev == number((along + d) % 4), old, new)
            mix[r64(along), cols] = jnp.where(dev == r, old, new)
        start(p4[s])

    def finish(s):
        arrive(p4[s])
        for cols in (ca(s), cb(s)):
            new = jnp.where(owner[...] == r, sel[:, cols], mix[:, cols])
            hi = new.astype(BF16)
            top_hi[:, cols] = hi
            top_lo[:, cols] = (new - hi.astype(F32)).astype(BF16)

    @pl.when((y == 0) & (x != 0))
    def _():
        tri_x[0].wait_recv()

    @pl.when(y == 0)
    def _():
        for cp in tri_y:
            cp.start()

    @pl.when(y != 0)
    def _():
        tri_y[0].wait_recv()

    for d in order:
        tri_z[d].start()
    tri_core[0].start()
    for d in late:
        pan_z[d].start()

    add_one(0)
    add_one(1)
    for d in order:
        tri_z[d].wait_recv()
        tri_core[d].start()
    add_two(0)
    add_two(1)
    for d in range(8):
        tri_core[d].wait_recv()
    stages = inverse_stages(tri, power, inv)
    for stage in stages[:3]:
        stage()
    last(0)
    stages[3]()
    last(1)
    for stage in stages[4:]:
        stage()
    for d in order:
        pan_z[d].wait_recv()
        pan_core[d].start()
    for d in range(8):
        pan_core[d].wait_recv()

    for m in range(ROWS // NB):
        w = exact(inv[...], pan[:, m * NB : (m + 1) * NB])
        if m == 0:
            w = jnp.where(is_root, -inv[...], w)
        w = jnp.transpose(w)
        hi = w.astype(BF16)
        w_hi[m * NB : (m + 1) * NB, :] = hi
        w_lo[m * NB : (m + 1) * NB, :] = (w - hi.astype(F32)).astype(BF16)

    for s in range(SUB):
        finish(s)
    for copies in p1 + p2 + p3 + p4 + [pan_z.values(), pan_core, tri_z.values(), tri_core]:
        for cp in copies:
            cp.wait_send()

    @pl.when(is_root)
    def _():
        for cp in tri_x:
            cp.wait_send()

    @pl.when(y == 0)
    def _():
        for cp in tri_y:
            cp.wait_send()


def exchange(pivots, matrix, panel):
    vmem = pl.BlockSpec(memory_space=pltpu.VMEM)
    hbm = pl.BlockSpec(memory_space=pltpu.HBM)
    dma = pltpu.SemaphoreType.DMA
    return pl.pallas_call(
        exchange_kernel,
        out_shape=(
            pltpu.VMEM((ROWS, COLS), F32),
            jax.ShapeDtypeStruct((NB, COLS), F32),
            jax.ShapeDtypeStruct((NB, COLS), BF16),
            jax.ShapeDtypeStruct((NB, COLS), BF16),
            jax.ShapeDtypeStruct((ROWS, NB), BF16),
            jax.ShapeDtypeStruct((ROWS, NB), BF16),
        ),
        in_specs=[hbm, hbm, hbm],
        out_specs=(vmem,) * 6,
        scratch_shapes=[
            pltpu.SMEM((NB,), jnp.int32),
            pltpu.VMEM((NB, WIDE), jnp.int32),
            pltpu.VMEM((NB, COLS), F32),
            pltpu.VMEM((SUB, 3, 64, WIDE), F32),
            pltpu.VMEM((SUB, 3, 64, WIDE), F32),
            pltpu.VMEM((SUB, 3, 16, WIDE), F32),
            pltpu.VMEM((SUB, 3, 16, WIDE), F32),
            pltpu.VMEM((SUB, 64, WIDE), F32),
            pltpu.VMEM((SUB, 64, WIDE), F32),
            pltpu.VMEM((SUB, 64, WIDE), F32),
            pltpu.VMEM((SUB, 64, WIDE), F32),
            pltpu.VMEM((SUB, 64, WIDE), F32),
            pltpu.VMEM((SUB, 64, WIDE), F32),
            pltpu.VMEM((SUB, 4, 2, 16, WIDE), F32),
            pltpu.VMEM((SUB, 4, 2, 16, WIDE), F32),
            pltpu.VMEM((SUB, 3, 64, WIDE), F32),
            pltpu.VMEM((SUB, 3, 64, WIDE), F32),
            pltpu.VMEM((NB, ROWS), F32),
            pltpu.VMEM((NB, NB), F32),
            pltpu.VMEM((NB, NB), F32),
            pltpu.VMEM((NB, NB), F32),
            dma((3,)),
            dma((6 * SUB,)), dma((6 * SUB,)), dma((6 * SUB,)), dma((6 * SUB,)),
            dma((6 * SUB,)), dma((6 * SUB,)), dma((6 * SUB,)), dma((6 * SUB,)),
            dma((6,)), dma((2,)),
            dma((7,)), dma((7,)), dma((8,)), dma((8,)),
            dma((7,)), dma((7,)), dma((8,)), dma((8,)),
        ],
        name="exchange",
        compiler_params=pltpu.CompilerParams(
            collective_id=0, has_side_effects=True, vmem_limit_bytes=24 * 1024 * 1024
        ),
    )(*(pltpu.with_memory_space_constraint(a, pltpu.HBM) for a in (pivots, matrix, panel)))


TILE = 256


def update_kernel(piv, mat, mix, th, tl, w_hi, w_lo, out_hbm, out, at_row, at_k, out_sem):
    r = lax.axis_index("row")
    tiles = ROWS // TILE

    def store(t):
        rows = pl.ds(t * TILE, TILE)
        return pltpu.make_async_copy(out.at[rows], out_hbm.at[rows], out_sem.at[t])

    first = r * ROWS

    def collect(g, n):
        for i in range(8):
            off = piv[g * 8 + i] - first
            at_row[n] = off
            at_k[n] = g * 8 + i
            n = n + jnp.where((off >= 0) & (off < ROWS), 1, 0)
        return n

    count = lax.fori_loop(0, NB // 8, collect, 0)

    def dot(a, b):
        return jnp.dot(a, b, preferred_element_type=F32)

    for t in range(tiles):
        rows = pl.ds(t * TILE, TILE)
        a, b = w_hi[rows, :], w_lo[rows, :]
        base = mat[rows, :]
        if t == 0:
            base = jnp.where(r == 0, 0.0, base)
        out[rows, :] = base - (dot(a, th[...]) + (dot(b, th[...]) + dot(a, tl[...])))

        def fix(n, carry):
            row = at_row[n]

            @pl.when((row >= t * TILE) & (row < (t + 1) * TILE))
            def _():
                one = pl.ds(row, 1)
                k = pl.ds(at_k[n], 1)
                old = jnp.where(r == 0, mat[k, :], mix[k, :])
                out[one, :] = out[one, :] + (old - mat[one, :])

            return carry

        lax.fori_loop(0, count, fix, 0)
        store(t).start()
    for t in range(tiles):
        store(t).wait()


def update(pivots, matrix, mix, top_hi, top_lo, w_hi, w_lo):
    vmem = pl.BlockSpec(memory_space=pltpu.VMEM)
    smem = pl.BlockSpec(memory_space=pltpu.SMEM)
    return pl.pallas_call(
        update_kernel,
        out_shape=jax.ShapeDtypeStruct((ROWS, COLS), F32),
        in_specs=[smem] + [vmem] * 6,
        out_specs=pl.BlockSpec(memory_space=pl.ANY),
        scratch_shapes=[
            pltpu.VMEM((ROWS, COLS), F32),
            pltpu.SMEM((NB + 8,), jnp.int32),
            pltpu.SMEM((NB + 8,), jnp.int32),
            pltpu.SemaphoreType.DMA((6,)),
        ],
        name="update",
        compiler_params=pltpu.CompilerParams(vmem_limit_bytes=24 * 1024 * 1024),
    )(pivots, matrix, mix, top_hi, top_lo, w_hi, w_lo)


def body(matrix, lower_panel, pivots):
    return update(pivots, *exchange(pivots, matrix, lower_panel))


def solution(mesh):
    placed = (P("row", "col"), P("col", "row"), P())
    return jax.shard_map(
        body, mesh=mesh, in_specs=placed, out_specs=P("row", "col"), check_vma=False
    )
```

time: 251 us -> 50.3 us (0.20)
  waiting for transfers between devices: 158 us -> 0 us
  Pallas kernels: 0 us -> 50.2 us
  matrix products: 28.9 us -> 0 us
  blocking collectives: 22 us -> 0 us
  local copies, waits for them, and re-layouts: 20.8 us -> 0.01 us
  between operations: 15.2 us -> 0.02 us
  other arithmetic: 5.01 us -> 0 us
    psum x2 -> x0, waiting for transfers between devices: 158 us -> none  [the longest x1 88.6 us: from_root(): return lax.psum(block, axis)]
    pallas_call x0 -> x2, Pallas kernels: none -> 50.2 us  [the longest x1 43 us: exchange(): pl.pallas_call(exchange_kernel, out_shape=(pltpu.VMEM((ROWS, COLS), F32),...]
    dot_general x80 -> x0, matrix products: 28.9 us -> none  [the longest x79 18.4 us: multiply(): jnp.dot(left_side, right_side, preferred_element_type=jnp.float32, precis...]
    all_gather x1 -> x0, blocking collectives: 22 us -> none  [body(): triangle = lax.all_gather(lower_panel[:, :NB], 'col', axis=0, tiled=True)]
    scatter x1 -> x0, local copies, waits for them, and re-layouts: 7.69 us -> none  [body(): matrix.at[slot_rows]]
    unnamed x7 -> x2, local copies, waits for them, and re-layouts: 6.63 us -> 0.01 us
    gather x1 -> x0, local copies, waits for them, and re-layouts: 5.61 us -> none  [body(): fetched = matrix[jnp.clip(offsets, 0, rows_dev - 1)]]
    select_n x3 -> x0, other arithmetic: 2.66 us -> none  [the longest x1 1.52 us: body(): moved_rows = lax.psum(jnp.where(owned_mask[:, None], fetched, 0.0), 'row')]
  transfers between devices with their start and end apart: 3 -> 0, of which waited for: 2 -> 0; matrix products, arithmetic and copies ran while one was open for 11% -> 0% of each run, Pallas kernels for 0% -> 0%
where the time goes in v2:
time: 50.3 us
  Pallas kernels  50.2 us (100%)
    pallas_call x1, Pallas kernels, exchange(): pl.pallas_call(exchange_kernel, out_shape=(pltpu.VMEM((ROWS, COLS), F32),...  43 us
    pallas_call x1, Pallas kernels, update(): pl.pallas_call(update_kernel, out_shape=jax.ShapeDtypeStruct((ROWS, COLS)...  7.27 us

profile of v2, /device:TPU:1, one launch (start us, length us, event | category | flops | bytes accessed | tf_op | source)
XLA Modules:
  0.0 50.3 jit_solution(16484280184068746400)
XLA Ops:
  0.0 0.0 copy-start
  0.0 43.0 %exchange.1 = (f32[1536,1024]{1,0:T(8,128)S(1)}, f32[256,1024]{1,0:T(8,128)S(1)}, bf16[256,1024]{1,0:T(8,128)(2,1)S(1)}, bf16[256,1024]{1,0:T(8,128)(2,1)S(1)}, ...) custom-call(s32[256]{0:T(256)} %piv.1, f32[1536,1024]{1,0:T(8,128)} %mat_hbm.1, f32[16,1536]{1,0:T(8,128)} %panel_hbm.1), custom_call_target="tpu_custom_call" | custom-call | tf_op jit(solution)/shard_map/exchange/pallas_call | solution.py:331
  43.0 0.0 copy-done
  43.0 7.3 %update.1 = f32[1536,1024]{1,0:T(8,128)} custom-call(s32[256]{0:T(256)S(1)} %copy-done, f32[1536,1024]{1,0:T(8,128)S(1)} %get-tuple-element.11.mat, f32[256,1024]{1,0:T(8,128)S(1)} %get-tuple-element.12.mix, bf16[256,1024]{1,0:T(8,128)(2,1)S(1)} %get-tuple-element.13.th, bf16[256,1024]{1,0:T(8,128)(2,1)S(1)} %get-tuple-element.14.tl, ...), custom_call_target="tpu_custom_call" | custom-call | tf_op jit(solution)/shard_map/update/pallas_call | solution.py:434
Async XLA Ops:
  0.0 43.0 %copy-start = (s32[256]{0:T(256)S(1)}, s32[256]{0:T(256)}, u32[]{:S(2)}) copy-start(s32[256]{0:T(256)} %piv.1) | copy-start | bytes 3076

commit v3 on v2

--- a/solution.py
+++ b/solution.py
@@ -43,12 +43,14 @@
 
 
 SUB = 2
+TILE = 256
+TILES = ROWS // TILE
 WIDE = HALF // SUB
 
 
 def exchange_kernel(
-    piv_hbm, mat_hbm, panel_hbm, mat, mix, top_hi, top_lo, w_hi, w_lo,
-    piv, owner, sel, r1a, r1b, r2a, r2b, pa, pb, ga, gb, sa, sb, both_a, both_b, m4a, m4b, pan, tri, power, inv,
+    piv_hbm, mat_hbm, panel_hbm, mat, lists, mix, top_hi, top_lo, w_hi, w_lo,
+    piv, column_of, owner, sel, r1a, r1b, r2a, r2b, pa, pb, ga, gb, sa, sb, both_a, both_b, m4a, m4b, pan, tri, power, inv,
     in_sem, p1s, p1r, p2s, p2r, p3s, p3r, p4s, p4r, tbs, tbr,
     tzs, tzr, tcs, tcr, pzs, pzr, pcs, pcr,
 ):
@@ -83,6 +85,24 @@
     for d in range(1, 8):
         pl.semaphore_signal(barrier, inc=1, device_id=coldev((z + d) % 8, k), device_id_type=MESH)
     pl.semaphore_signal(barrier, inc=1, device_id=coldev(z, 1 - k), device_id_type=MESH)
+
+
+    load_piv.wait()
+    load_mat.wait()
+    first = r * ROWS
+
+    def pick(g, carry):
+        for i in range(8):
+            at = pl.ds(g * 8 + i, 1)
+            pivot = piv[g * 8 + i]
+            off = pivot - first
+            own = (off >= 0) & (off < ROWS)
+            row = mat[pl.ds(jnp.clip(off, 0, ROWS - 1), 1), :]
+            sel[at, :] = jnp.where(own, row, jnp.where(is_root, mat[at, :], 0.0))
+            column_of[at, :] = jnp.full((1, WIDE), pivot, jnp.int32)
+        return carry
+
+    lax.fori_loop(0, NB // 16, pick, 0)
     pl.semaphore_wait(barrier, 14)
 
     def remote(src, dst, ss, rs, dev):
@@ -125,28 +145,26 @@
 
     tri_z, tri_core = column(tri, tzs, tzr, tcs, tcr)
     pan_z, pan_core = column(pan, pzs, pzr, pcs, pcr)
-    early, late = (1, 7, 2, 6), (3, 5, 4)
-    order = early + late
+    early = (1, 7, 2, 6)
+    order = early + (3, 5, 4)
+    for d, held, step in ((3, 2, 1), (5, 6, 7), (4, 2, 2)):
+        got = piece(pan, (z + 8 - held) % 8, k)
+        pan_z[d] = remote(got, got, pzs.at[d - 1], pzr.at[d - 1], coldev((z + step) % 8, k))
     for d in early:
         pan_z[d].start()
     pan_core[0].start()
 
-    load_piv.wait()
-    load_mat.wait()
-    first = r * ROWS
-
-    def pick(g, carry):
-        for i in range(8):
-            at = pl.ds(g * 8 + i, 1)
-            pivot = piv[g * 8 + i]
-            off = pivot - first
-            own = (off >= 0) & (off < ROWS)
-            row = mat[pl.ds(jnp.clip(off, 0, ROWS - 1), 1), :]
-            sel[at, :] = jnp.where(own, row, jnp.where(is_root, mat[at, :], 0.0))
-            owner[at, :] = jnp.full((1, WIDE), ((pivot >> 9) * 43691) >> 17, jnp.int32)
-        return carry
-
-    lax.fori_loop(0, NB // 8, pick, 0)
+    lax.fori_loop(NB // 16, NB // 8, pick, 0)
+    owner[...] = ((column_of[...] >> 9) * 43691) >> 17
+
+    @pl.when((y == 0) & (x != 0))
+    def _():
+        tri_x[0].wait_recv()
+
+    @pl.when(y == 0)
+    def _():
+        for cp in tri_y:
+            cp.start()
 
     def ca(s):
         return pl.ds(s * WIDE, WIDE)
@@ -256,15 +274,6 @@
             top_hi[:, cols] = hi
             top_lo[:, cols] = (new - hi.astype(F32)).astype(BF16)
 
-    @pl.when((y == 0) & (x != 0))
-    def _():
-        tri_x[0].wait_recv()
-
-    @pl.when(y == 0)
-    def _():
-        for cp in tri_y:
-            cp.start()
-
     @pl.when(y != 0)
     def _():
         tri_y[0].wait_recv()
@@ -272,14 +281,29 @@
     for d in order:
         tri_z[d].start()
     tri_core[0].start()
-    for d in late:
+    for d in (2, 6):
+        pan_z[d].wait_recv()
+        pan_core[d].start()
+    for d in (3, 5, 4):
         pan_z[d].start()
 
+    local = column_of[...] - first
+    number = lax.broadcasted_iota(jnp.int32, (NB, NB), 0)
+    slot = lax.broadcasted_iota(jnp.int32, (NB, NB), 1)
+    before = jnp.where(number > slot, 1.0, 0.0).astype(BF16)
+    lists[...] = jnp.zeros_like(lists)
+    for t in range(TILES):
+        inside = (local >= t * TILE) & (local < (t + 1) * TILE)
+        rank = jnp.dot(before, jnp.where(inside, 1.0, 0.0).astype(BF16), preferred_element_type=F32)
+        packed = jnp.where(inside & (rank.astype(jnp.int32) == slot), local * NB + number, 0)
+        lists[t : t + 1, :] = jnp.sum(packed, axis=0, keepdims=True)
+        lists[8 + t : 9 + t, :] = jnp.sum(jnp.where(inside, 1, 0), axis=0, keepdims=True)
+
     add_one(0)
-    add_one(1)
     for d in order:
         tri_z[d].wait_recv()
         tri_core[d].start()
+    add_one(1)
     add_two(0)
     add_two(1)
     for d in range(8):
@@ -292,7 +316,7 @@
     last(1)
     for stage in stages[4:]:
         stage()
-    for d in order:
+    for d in (1, 7, 3, 5, 4):
         pan_z[d].wait_recv()
         pan_core[d].start()
     for d in range(8):
@@ -332,6 +356,7 @@
         exchange_kernel,
         out_shape=(
             pltpu.VMEM((ROWS, COLS), F32),
+            jax.ShapeDtypeStruct((16, NB), jnp.int32),
             jax.ShapeDtypeStruct((NB, COLS), F32),
             jax.ShapeDtypeStruct((NB, COLS), BF16),
             jax.ShapeDtypeStruct((NB, COLS), BF16),
@@ -339,9 +364,10 @@
             jax.ShapeDtypeStruct((ROWS, NB), BF16),
         ),
         in_specs=[hbm, hbm, hbm],
-        out_specs=(vmem,) * 6,
+        out_specs=(vmem,) * 7,
         scratch_shapes=[
             pltpu.SMEM((NB,), jnp.int32),
+            pltpu.VMEM((NB, WIDE), jnp.int32),
             pltpu.VMEM((NB, WIDE), jnp.int32),
             pltpu.VMEM((NB, COLS), F32),
             pltpu.VMEM((SUB, 3, 64, WIDE), F32),
@@ -376,79 +402,62 @@
     )(*(pltpu.with_memory_space_constraint(a, pltpu.HBM) for a in (pivots, matrix, panel)))
 
 
-TILE = 256
-
-
-def update_kernel(piv, mat, mix, th, tl, w_hi, w_lo, out_hbm, out, at_row, at_k, out_sem):
+def update_kernel(mat, lists, mix, th, tl, w_hi, w_lo, out_hbm, out, swaps, list_sem, out_sem):
     r = lax.axis_index("row")
-    tiles = ROWS // TILE
+    load = pltpu.make_async_copy(lists, swaps, list_sem)
+    load.start()
 
     def store(t):
         rows = pl.ds(t * TILE, TILE)
         return pltpu.make_async_copy(out.at[rows], out_hbm.at[rows], out_sem.at[t])
 
-    first = r * ROWS
-
-    def collect(g, n):
-        for i in range(8):
-            off = piv[g * 8 + i] - first
-            at_row[n] = off
-            at_k[n] = g * 8 + i
-            n = n + jnp.where((off >= 0) & (off < ROWS), 1, 0)
-        return n
-
-    count = lax.fori_loop(0, NB // 8, collect, 0)
-
     def dot(a, b):
         return jnp.dot(a, b, preferred_element_type=F32)
 
-    for t in range(tiles):
+    for t in range(TILES):
         rows = pl.ds(t * TILE, TILE)
         a, b = w_hi[rows, :], w_lo[rows, :]
         base = mat[rows, :]
         if t == 0:
             base = jnp.where(r == 0, 0.0, base)
         out[rows, :] = base - (dot(a, th[...]) + (dot(b, th[...]) + dot(a, tl[...])))
+        if t == 0:
+            load.wait()
 
         def fix(n, carry):
-            row = at_row[n]
-
-            @pl.when((row >= t * TILE) & (row < (t + 1) * TILE))
-            def _():
-                one = pl.ds(row, 1)
-                k = pl.ds(at_k[n], 1)
-                old = jnp.where(r == 0, mat[k, :], mix[k, :])
-                out[one, :] = out[one, :] + (old - mat[one, :])
-
+            entry = swaps[t, n]
+            one, k = pl.ds(entry >> 8, 1), pl.ds(entry & (NB - 1), 1)
+            old = jnp.where(r == 0, mat[k, :], mix[k, :])
+            out[one, :] = out[one, :] + (old - mat[one, :])
             return carry
 
-        lax.fori_loop(0, count, fix, 0)
+        lax.fori_loop(0, swaps[8 + t, 0], fix, 0)
         store(t).start()
-    for t in range(tiles):
+    for t in range(TILES):
         store(t).wait()
 
 
-def update(pivots, matrix, mix, top_hi, top_lo, w_hi, w_lo):
+def update(matrix, lists, mix, top_hi, top_lo, w_hi, w_lo):
     vmem = pl.BlockSpec(memory_space=pltpu.VMEM)
-    smem = pl.BlockSpec(memory_space=pltpu.SMEM)
+    anyspace = pl.BlockSpec(memory_space=pl.ANY)
     return pl.pallas_call(
         update_kernel,
         out_shape=jax.ShapeDtypeStruct((ROWS, COLS), F32),
-        in_specs=[smem] + [vmem] * 6,
-        out_specs=pl.BlockSpec(memory_space=pl.ANY),
+        in_specs=[vmem, anyspace] + [vmem] * 5,
+        out_specs=anyspace,
         scratch_shapes=[
             pltpu.VMEM((ROWS, COLS), F32),
-            pltpu.SMEM((NB + 8,), jnp.int32),
-            pltpu.SMEM((NB + 8,), jnp.int32),
-            pltpu.SemaphoreType.DMA((6,)),
+            pltpu.SMEM((16, NB), jnp.int32),
+            pltpu.SemaphoreType.DMA,
+            pltpu.SemaphoreType.DMA((TILES,)),
         ],
         name="update",
         compiler_params=pltpu.CompilerParams(vmem_limit_bytes=24 * 1024 * 1024),
-    )(pivots, matrix, mix, top_hi, top_lo, w_hi, w_lo)
+    )(matrix, lists, mix, top_hi, top_lo, w_hi, w_lo)
 
 
 def body(matrix, lower_panel, pivots):
-    return update(pivots, *exchange(pivots, matrix, lower_panel))
+    return update(*exchange(pivots, matrix, lower_panel))
 
 
 def solution(mesh):

time: 50.3 us -> 48.2 us (0.958)
  Pallas kernels: 50.2 us -> 48.1 us
    pallas_call x1, Pallas kernels: 7.27 us -> 4.82 us  [update(): pl.pallas_call(update_kernel, out_shape=jax.ShapeDtypeStruct((ROWS, COLS)...]
where the time goes in v3:
time: 48.2 us; the launch traced here: 48.1 us
  Pallas kernels  48.1 us (100%)
    pallas_call x1, Pallas kernels, exchange(): pl.pallas_call(exchange_kernel, out_shape=(pltpu.VMEM((ROWS, COLS), F32),...  43.3 us
    pallas_call x1, Pallas kernels, update(): pl.pallas_call(update_kernel, out_shape=jax.ShapeDtypeStruct((ROWS, COLS)...  4.82 us

profile of v3, /device:TPU:1, one launch (start us, length us, event | category | flops | bytes accessed | tf_op | source)
XLA Modules:
  0.0 48.1 jit_solution(9595884351005186532)
XLA Ops:
  0.0 43.3 %exchange.1 = (f32[1536,1024]{1,0:T(8,128)S(1)}, s32[16,256]{1,0:T(8,128)S(1)}, f32[256,1024]{1,0:T(8,128)S(1)}, bf16[256,1024]{1,0:T(8,128)(2,1)S(1)}, bf16[256...) custom-call(s32[256]{0:T(256)} %piv_hbm.1, f32[1536,1024]{1,0:T(8,128)} %mat_hbm.1, ...), custom_call_target="tpu_custom_call" | custom-call | tf_op jit(solution)/shard_map/exchange/pallas_call | solution.py:355
  43.3 4.8 %update.1 = f32[1536,1024]{1,0:T(8,128)} custom-call(f32[1536,1024]{1,0:T(8,128)S(1)} %get-tuple-element.12.mat, s32[16,256]{1,0:T(8,128)S(1)} %get-tuple-element.13.lists, f32[256,1024]{1,0:T(8,128)S(1)} %get-tuple-element.14.mix, bf16[256,1024]{1,0:T(8,128)(2,1)S(1)} %get-tuple-element.15.th, bf16[256,1024]{1,0:T(8,128)(2,1)S(1)} %get-tuple-element.16.tl, ...), custom_call_target="tpu_custom_call" | custom-call | tf_op jit(solution)/shard_map/update/pallas_call | solution.py:443

commit v4 on v3

--- a/solution.py
+++ b/solution.py
@@ -20,6 +20,13 @@
     return jnp.dot(a, b, preferred_element_type=F32, precision=lax.Precision.HIGHEST)
 
 
+def three_pass(a_hi, a_lo, b_hi, b_lo):
+    def dot(a, b):
+        return jnp.dot(a, b, preferred_element_type=F32)
+
+    return dot(a_hi, b_hi) + (dot(a_lo, b_hi) + dot(a_hi, b_lo))
+
+
 def inverse_stages(tri, power, inv):
     i = lax.broadcasted_iota(jnp.int32, (NB, NB), 0)
     j = lax.broadcasted_iota(jnp.int32, (NB, NB), 1)
@@ -49,7 +56,7 @@
 
 
 def exchange_kernel(
-    piv_hbm, mat_hbm, panel_hbm, mat, lists, mix, top_hi, top_lo, w_hi, w_lo,
+    piv_hbm, mat_hbm, panel_hbm, mat, lists, product, mix, top_hi, top_lo, w_hi, w_lo,
     piv, column_of, owner, sel, r1a, r1b, r2a, r2b, pa, pb, ga, gb, sa, sb, both_a, both_b, m4a, m4b, pan, tri, power, inv,
     in_sem, p1s, p1r, p2s, p2r, p3s, p3r, p4s, p4r, tbs, tbr,
     tzs, tzr, tcs, tcr, pzs, pzr, pcs, pcr,
@@ -85,6 +92,10 @@
     for d in range(1, 8):
         pl.semaphore_signal(barrier, inc=1, device_id=coldev((z + d) % 8, k), device_id_type=MESH)
     pl.semaphore_signal(barrier, inc=1, device_id=coldev(z, 1 - k), device_id_type=MESH)
+
+    @pl.when((x != 0) & (y != 0))
+    def _():
+        pl.semaphore_signal(barrier, inc=1, device_id=(0, c), device_id_type=MESH)
 
 
     load_piv.wait()
@@ -103,7 +114,7 @@
         return carry
 
     lax.fori_loop(0, NB // 16, pick, 0)
-    pl.semaphore_wait(barrier, 14)
+    pl.semaphore_wait(barrier, jnp.where(is_root, 23, 14))
 
     def remote(src, dst, ss, rs, dev):
         return pltpu.make_async_remote_copy(
@@ -122,14 +133,13 @@
     near = (1, 3, 2)
 
     load_pan.wait()
-    tri_x = [
-        remote(my_pan.at[:, pl.ds(0, NB)], my_tri, tbs.at[d - 1], tbr.at[0], rowdev(y, (x + d) % 4)) for d in range(1, 4)
+    tri_all = [
+        remote(my_pan.at[:, pl.ds(0, NB)], my_tri, tbs.at[d - 1], tbr.at[0], ((r + d) % 16, c)) for d in range(1, 16)
     ]
-    tri_y = [remote(my_tri, my_tri, tbs.at[d + 2], tbr.at[1], rowdev((y + d) % 4, x)) for d in range(1, 4)]
 
     @pl.when(is_root)
     def _():
-        for cp in tri_x:
+        for cp in tri_all:
             cp.start()
         mine = pl.ds(pl.multiple_of(c * 16, 16), 16)
         tri[mine, :] = pan[mine, :NB]
@@ -145,26 +155,16 @@
 
     tri_z, tri_core = column(tri, tzs, tzr, tcs, tcr)
     pan_z, pan_core = column(pan, pzs, pzr, pcs, pcr)
-    early = (1, 7, 2, 6)
-    order = early + (3, 5, 4)
+    order = (1, 7, 2, 6, 3, 5, 4)
     for d, held, step in ((3, 2, 1), (5, 6, 7), (4, 2, 2)):
         got = piece(pan, (z + 8 - held) % 8, k)
         pan_z[d] = remote(got, got, pzs.at[d - 1], pzr.at[d - 1], coldev((z + step) % 8, k))
-    for d in early:
+    for d in (1, 7, 2, 6):
         pan_z[d].start()
     pan_core[0].start()
 
     lax.fori_loop(NB // 16, NB // 8, pick, 0)
     owner[...] = ((column_of[...] >> 9) * 43691) >> 17
-
-    @pl.when((y == 0) & (x != 0))
-    def _():
-        tri_x[0].wait_recv()
-
-    @pl.when(y == 0)
-    def _():
-        for cp in tri_y:
-            cp.start()
 
     def ca(s):
         return pl.ds(s * WIDE, WIDE)
@@ -187,6 +187,11 @@
     def start(copies):
         for cp in copies:
             cp.start()
+
+    def left(groups):
+        for copies in groups:
+            for cp in copies:
+                cp.wait_send()
 
     def arrive(copies):
         for cp in copies:
@@ -210,7 +215,6 @@
             s, p4s, p4r,
             lambda to, d: (m4a.at[s, d], mix.at[r64(x), ca(s)]),
             lambda to, d: (m4b.at[s, d], mix.at[r64(y), cb(s)]), True))
-        start(p1[s])
 
     def total(parts, here, foreign):
         out = None
@@ -274,19 +278,16 @@
             top_hi[:, cols] = hi
             top_lo[:, cols] = (new - hi.astype(F32)).astype(BF16)
 
-    @pl.when(y != 0)
+    start(p1[0])
+    start(p1[1])
+
+    @pl.when(r != 0)
     def _():
-        tri_y[0].wait_recv()
+        tri_all[0].wait_recv()
 
     for d in order:
         tri_z[d].start()
     tri_core[0].start()
-    for d in (2, 6):
-        pan_z[d].wait_recv()
-        pan_core[d].start()
-    for d in (3, 5, 4):
-        pan_z[d].start()
-
     local = column_of[...] - first
     number = lax.broadcasted_iota(jnp.int32, (NB, NB), 0)
     slot = lax.broadcasted_iota(jnp.int32, (NB, NB), 1)
@@ -299,26 +300,43 @@
         lists[t : t + 1, :] = jnp.sum(packed, axis=0, keepdims=True)
         lists[8 + t : 9 + t, :] = jnp.sum(jnp.where(inside, 1, 0), axis=0, keepdims=True)
 
+    for d in (2, 6):
+        pan_z[d].wait_recv()
+        pan_core[d].start()
+    for d in (3, 5, 4):
+        pan_z[d].start()
     add_one(0)
     for d in order:
         tri_z[d].wait_recv()
         tri_core[d].start()
     add_one(1)
+    left(p1)
+    for d in (1, 7):
+        pan_z[d].wait_recv()
+        pan_core[d].start()
     add_two(0)
     add_two(1)
+    left(p2)
     for d in range(8):
         tri_core[d].wait_recv()
+    left([tri_z.values(), tri_core])
+
+    @pl.when(is_root)
+    def _():
+        left([tri_all])
+
     stages = inverse_stages(tri, power, inv)
     for stage in stages[:3]:
         stage()
     last(0)
     stages[3]()
     last(1)
+    left(p3)
+    for d in (3, 5, 4):
+        pan_z[d].wait_recv()
+        pan_core[d].start()
     for stage in stages[4:]:
         stage()
-    for d in (1, 7, 3, 5, 4):
-        pan_z[d].wait_recv()
-        pan_core[d].start()
     for d in range(8):
         pan_core[d].wait_recv()
 
@@ -331,21 +349,14 @@
         w_hi[m * NB : (m + 1) * NB, :] = hi
         w_lo[m * NB : (m + 1) * NB, :] = (w - hi.astype(F32)).astype(BF16)
 
-    for s in range(SUB):
-        finish(s)
-    for copies in p1 + p2 + p3 + p4 + [pan_z.values(), pan_core, tri_z.values(), tri_core]:
-        for cp in copies:
-            cp.wait_send()
-
-    @pl.when(is_root)
-    def _():
-        for cp in tri_x:
-            cp.wait_send()
-
-    @pl.when(y == 0)
-    def _():
-        for cp in tri_y:
-            cp.wait_send()
+    left([pan_z.values(), pan_core])
+    finish(0)
+    for t in range(TILES):
+        rows = pl.ds(t * TILE, TILE)
+        for n, cols in enumerate((ca(0), cb(0))):
+            product[rows, n * WIDE : (n + 1) * WIDE] = three_pass(w_hi[rows, :], w_lo[rows, :], top_hi[:, cols], top_lo[:, cols])
+    finish(1)
+    left(p4)
 
 
 def exchange(pivots, matrix, panel):
@@ -357,6 +368,7 @@
         out_shape=(
             pltpu.VMEM((ROWS, COLS), F32),
             jax.ShapeDtypeStruct((16, NB), jnp.int32),
+            jax.ShapeDtypeStruct((ROWS, HALF), F32),
             jax.ShapeDtypeStruct((NB, COLS), F32),
             jax.ShapeDtypeStruct((NB, COLS), BF16),
             jax.ShapeDtypeStruct((NB, COLS), BF16),
@@ -364,7 +376,7 @@
             jax.ShapeDtypeStruct((ROWS, NB), BF16),
         ),
         in_specs=[hbm, hbm, hbm],
-        out_specs=(vmem,) * 7,
+        out_specs=(vmem,) * 8,
         scratch_shapes=[
             pltpu.SMEM((NB,), jnp.int32),
             pltpu.VMEM((NB, WIDE), jnp.int32),
@@ -391,7 +403,7 @@
             dma((3,)),
             dma((6 * SUB,)), dma((6 * SUB,)), dma((6 * SUB,)), dma((6 * SUB,)),
             dma((6 * SUB,)), dma((6 * SUB,)), dma((6 * SUB,)), dma((6 * SUB,)),
-            dma((6,)), dma((2,)),
+            dma((15,)), dma((1,)),
             dma((7,)), dma((7,)), dma((8,)), dma((8,)),
             dma((7,)), dma((7,)), dma((8,)), dma((8,)),
         ],
@@ -402,7 +414,7 @@
     )(*(pltpu.with_memory_space_constraint(a, pltpu.HBM) for a in (pivots, matrix, panel)))
 
 
-def update_kernel(mat, lists, mix, th, tl, w_hi, w_lo, out_hbm, out, swaps, list_sem, out_sem):
+def update_kernel(mat, lists, product, mix, th, tl, w_hi, w_lo, out_hbm, out, swaps, list_sem, out_sem):
     r = lax.axis_index("row")
     load = pltpu.make_async_copy(lists, swaps, list_sem)
     load.start()
@@ -411,16 +423,18 @@
         rows = pl.ds(t * TILE, TILE)
         return pltpu.make_async_copy(out.at[rows], out_hbm.at[rows], out_sem.at[t])
 
-    def dot(a, b):
-        return jnp.dot(a, b, preferred_element_type=F32)
-
     for t in range(TILES):
         rows = pl.ds(t * TILE, TILE)
-        a, b = w_hi[rows, :], w_lo[rows, :]
-        base = mat[rows, :]
-        if t == 0:
-            base = jnp.where(r == 0, 0.0, base)
-        out[rows, :] = base - (dot(a, th[...]) + (dot(b, th[...]) + dot(a, tl[...])))
+        for n in range(2):
+            for part in range(SUB):
+                cols = pl.ds(n * HALF + part * WIDE, WIDE)
+                base = mat[rows, cols]
+                if t == 0:
+                    base = jnp.where(r == 0, 0.0, base)
+                if part == 0:
+                    out[rows, cols] = base - product[rows, n * WIDE : (n + 1) * WIDE]
+                else:
+                    out[rows, cols] = base - three_pass(w_hi[rows, :], w_lo[rows, :], th[:, cols], tl[:, cols])
         if t == 0:
             load.wait()
 
@@ -437,13 +451,13 @@
         store(t).wait()
 
 
-def update(matrix, lists, mix, top_hi, top_lo, w_hi, w_lo):
+def update(matrix, lists, product, mix, top_hi, top_lo, w_hi, w_lo):
     vmem = pl.BlockSpec(memory_space=pltpu.VMEM)
     anyspace = pl.BlockSpec(memory_space=pl.ANY)
     return pl.pallas_call(
         update_kernel,
         out_shape=jax.ShapeDtypeStruct((ROWS, COLS), F32),
-        in_specs=[vmem, anyspace] + [vmem] * 5,
+        in_specs=[vmem, anyspace] + [vmem] * 6,
         out_specs=anyspace,
         scratch_shapes=[
             pltpu.VMEM((ROWS, COLS), F32),
@@ -453,7 +467,7 @@
         ],
         name="update",
         compiler_params=pltpu.CompilerParams(vmem_limit_bytes=24 * 1024 * 1024),
-    )(matrix, lists, mix, top_hi, top_lo, w_hi, w_lo)
+    )(matrix, lists, product, mix, top_hi, top_lo, w_hi, w_lo)
 
 
 def body(matrix, lower_panel, pivots):

time: 48.2 us -> 45.4 us (0.942)
  Pallas kernels: 48.1 us -> 45.1 us
    pallas_call x1, Pallas kernels: 43.3 us -> 41.1 us  [exchange(): pl.pallas_call(exchange_kernel, out_shape=(pltpu.VMEM((ROWS, COLS), F32),...]
    pallas_call x1, Pallas kernels: 4.82 us -> 3.94 us  [update(): pl.pallas_call(update_kernel, out_shape=jax.ShapeDtypeStruct((ROWS, COLS)...]
where the time goes in v4:
time: 45.4 us; the launch traced here: 45.1 us
  Pallas kernels  45.1 us (99%)
    pallas_call x1, Pallas kernels, exchange(): pl.pallas_call(exchange_kernel, out_shape=(pltpu.VMEM((ROWS, COLS), F32),...  41.1 us
    pallas_call x1, Pallas kernels, update(): pl.pallas_call(update_kernel, out_shape=jax.ShapeDtypeStruct((ROWS, COLS)...  3.94 us

profile of v4, /device:TPU:1, one launch (start us, length us, event | category | flops | bytes accessed | tf_op | source)
XLA Modules:
  0.0 45.1 jit_solution(11303618346608991243)
XLA Ops:
  0.0 41.1 %exchange.1 = (f32[1536,1024]{1,0:T(8,128)S(1)}, s32[16,256]{1,0:T(8,128)S(1)}, f32[1536,512]{1,0:T(8,128)S(1)}, f32[256,1024]{1,0:T(8,128)S(1)}, bf16[256,1024]...) custom-call(s32[256]{0:T(256)} %piv_hbm.1, ...), custom_call_target="tpu_custom_call" | custom-call | tf_op jit(solution)/shard_map/exchange/pallas_call | solution.py:366
  41.1 3.9 %update.1 = f32[1536,1024]{1,0:T(8,128)} custom-call(f32[1536,1024]{1,0:T(8,128)S(1)} %get-tuple-element.13.mat, s32[16,256]{1,0:T(8,128)S(1)} %get-tuple-element.14.lists, f32[1536,512]{1,0:T(8,128)S(1)} %get-tuple-element.15.product, f32[256,1024]{1,0:T(8,128)S(1)} %get-tuple-element.16.mix, bf16[256,1024]{1,0:T(8,128)(2,1)S(1)} %get-tuple-element.17.th, ...), custom_call_target="tpu_custom_call" | custom-call | tf_op jit(solution)/shard_map/update/pallas_call | solution.py:457

commit v5 on v4

--- a/solution.py
+++ b/solution.py
@@ -45,8 +45,12 @@
         block = (i // (2 * size) == j // (2 * size)) & (i // size < j // size)
         inv[...] = inv[...] - exact(exact(inv[...], jnp.where(block, tri[...], 0.0)), inv[...])
 
+    def join():
+        half = NB // 2
+        inv[:half, half:] = -exact(exact(inv[:half, :half], tri[:half, half:]), inv[half:, half:])
+
     steps = [begin, square, square, square, square]
-    return steps + [functools.partial(double, size) for size in (32, 64, 128)]
+    return steps + [functools.partial(double, size) for size in (32, 64)] + [join]
 
 
 SUB = 2
@@ -306,10 +310,10 @@
     for d in (3, 5, 4):
         pan_z[d].start()
     add_one(0)
+    add_one(1)
     for d in order:
         tri_z[d].wait_recv()
         tri_core[d].start()
-    add_one(1)
     left(p1)
     for d in (1, 7):
         pan_z[d].wait_recv()

time: 45.4 us -> 42.8 us (0.943)
  Pallas kernels: 45.1 us -> 42.1 us
    pallas_call x1, Pallas kernels: 41.1 us -> 38.1 us  [exchange(): pl.pallas_call(exchange_kernel, out_shape=(pltpu.VMEM((ROWS, COLS), F32),...]
where the time goes in v5:
time: 42.8 us; the launch traced here: 42.1 us
  Pallas kernels  42.1 us (98%)
    pallas_call x1, Pallas kernels, exchange(): pl.pallas_call(exchange_kernel, out_shape=(pltpu.VMEM((ROWS, COLS), F32),...  38.1 us
    pallas_call x1, Pallas kernels, update(): pl.pallas_call(update_kernel, out_shape=jax.ShapeDtypeStruct((ROWS, COLS)...  3.93 us

profile of v5, /device:TPU:1, one launch (start us, length us, event | category | flops | bytes accessed | tf_op | source)
XLA Modules:
  0.0 42.1 jit_solution(8257056954819703372)
XLA Ops:
  0.0 38.1 %exchange.1 = (f32[1536,1024]{1,0:T(8,128)S(1)}, s32[16,256]{1,0:T(8,128)S(1)}, f32[1536,512]{1,0:T(8,128)S(1)}, f32[256,1024]{1,0:T(8,128)S(1)}, bf16[256,1024]...) custom-call(s32[256]{0:T(256)} %piv_hbm.1, ...), custom_call_target="tpu_custom_call" | custom-call | tf_op jit(solution)/shard_map/exchange/pallas_call | solution.py:370
  38.1 3.9 %update.1 = f32[1536,1024]{1,0:T(8,128)} custom-call(f32[1536,1024]{1,0:T(8,128)S(1)} %get-tuple-element.13.mat, s32[16,256]{1,0:T(8,128)S(1)} %get-tuple-element.14.lists, f32[1536,512]{1,0:T(8,128)S(1)} %get-tuple-element.15.product, f32[256,1024]{1,0:T(8,128)S(1)} %get-tuple-element.16.mix, bf16[256,1024]{1,0:T(8,128)(2,1)S(1)} %get-tuple-element.17.th, ...), custom_call_target="tpu_custom_call" | custom-call | tf_op jit(solution)/shard_map/update/pallas_call | solution.py:461
